TPU v7x, 512 devices: a whole 4x4x16 slice. The times are simulated.
512 devices in a mesh: bin: 32 (over y, x, core), pen: 16 (over z).
Axes of the slice: x: 4, y: 4, z: 16, core: 2. Of those that a mesh axis runs over, the one named last changes fastest.
Arguments:
- features: bfloat16 [1048576, 64], P(('bin', 'pen')), may hold values from -6 to 6
- positions: float32 [3, 1048576], P(None, ('bin', 'pen')), may hold values from 0 to 192, as said below
- home_cells: int32 [3, 1048576], P(None, ('bin', 'pen')), may hold values from 0 to 191, as said below
- neighbours: int32 [1048576, 16], P(('bin', 'pen')), may hold values from 0 to 26, as said below
- degrees: int32 [1048576], P(('bin', 'pen')), may hold values from 1 to 16
- lift_input: bfloat16 [64, 64], replicated, may hold values from -0.75 to 0.75
- kernel_first: float32 [3, 64], replicated, may hold values from -4 to 4
- kernel_bias: float32 [64], replicated, may hold values from -1 to 1
- kernel_second: bfloat16 [64, 64], replicated, may hold values from -0.75 to 0.75
- spectral_weights: bfloat16 [32, 32, 32, 64, 128], P(None, 'bin', 'pen'), may hold values from -6 to 6
- skip_weights: float32 [64, 64], replicated, may hold values from -0.75 to 0.75
- skip_bias: float32 [64], replicated, may hold values from -0.5 to 0.5
Outputs:
- latent_out: bfloat16 [128, 128, 192, 64], P('bin', 'pen')
Inputs may be any that keep to these rules, and one draw needn't show every extreme that they name: `neighbours`: each code k names the step (k // 9 - 1, (k // 3) % 3 - 1, k % 3 - 1) of the 3 x 3 x 3 cells around a point's home cell; slot 0 is 13, the home cell itself, and the other slots hold distinct codes other than 13. `home_cells`: row 0 is below 4, row 1 below 8, row 2 below 192. `positions`: each point lies in its home cell: the integer parts of its coordinates are that cell's global coordinates.
All inputs are finite; a program needn't handle non-finite values.
Results may differ from a plain program's by a relative error of at most 0.0037.
Values sent between devices are 32-bit elements; how exact they have to be, the bound alone decides.
No kernel may reach another device: no remote copies, remote signals or barrier semaphores. Data moves between devices by JAX's collectives and lax.ppermute only.
A program may use at most 128 MiB of HBM per device.

v0:
```python
import math
import jax
import jax.numpy as jnp
from jax import lax
from jax.sharding import PartitionSpec as P

NZ = 192
CX = 4
CY = 8


def passed_along(block, axis, distance):
    devices = range(lax.axis_size(axis))
    route = [(i - distance, i) for i in devices if i - distance in devices]
    return lax.ppermute(block, axis, route)


def dft_table(rows, length, count, signed):
    mode = jnp.arange(count, dtype=jnp.int32)
    if signed:
        mode = jnp.where(mode < count // 2, mode, mode - count)
    phase = rows[:, None] * mode[None, :] % length
    angle = phase.astype(jnp.float32) * (2.0 * math.pi / length)
    scale = 1.0 / math.sqrt(length)
    return (jnp.cos(angle) * scale, jnp.sin(angle) * scale)


def pair_messages(
    off_x, off_y, off_z, feat_rows, valid, kernel_first, kernel_bias, kernel_second, lift_input
):
    pre = (
        off_x[..., None] * kernel_first[0]
        + off_y[..., None] * kernel_first[1]
        + off_z[..., None] * kernel_first[2]
        + kernel_bias
    )
    hidden = jax.nn.gelu(pre).astype(jnp.bfloat16)
    count, slots_n, width = hidden.shape
    kernel = jnp.dot(
        hidden.reshape(count * slots_n, width), kernel_second, preferred_element_type=jnp.float32
    )
    kernel = kernel.reshape(count, slots_n, -1)
    values = jnp.dot(feat_rows, lift_input, preferred_element_type=jnp.float32)
    return kernel * values[:, None, :] * valid[..., None]


def invert_along(spec, cos_t, sin_t, form):
    real = spec[:, :, :, 0]
    imag = spec[:, :, :, 1]
    high = lax.Precision.HIGHEST
    out_re = jnp.einsum(form, real, cos_t, precision=high) - jnp.einsum(
        form, imag, sin_t, precision=high
    )
    out_im = jnp.einsum(form, imag, cos_t, precision=high) + jnp.einsum(
        form, real, sin_t, precision=high
    )
    return jnp.stack([out_re, out_im], axis=3)


def forward_along(spec, cos_t, sin_t, form):
    real = spec[:, :, :, 0]
    imag = spec[:, :, :, 1]
    high = lax.Precision.HIGHEST
    out_re = jnp.einsum(form, real, cos_t, precision=high) + jnp.einsum(
        form, imag, sin_t, precision=high
    )
    out_im = jnp.einsum(form, imag, cos_t, precision=high) - jnp.einsum(
        form, real, sin_t, precision=high
    )
    return jnp.stack([out_re, out_im], axis=3)


def per_device(
    features,
    positions,
    home_cells,
    neighbours,
    degrees,
    lift_input,
    kernel_first,
    kernel_bias,
    kernel_second,
    spectral_weights,
    skip_weights,
    skip_bias,
):
    high = lax.Precision.HIGHEST
    bins = lax.axis_size("bin")
    pens = lax.axis_size("pen")
    bin_index = lax.axis_index("bin")
    pen_index = lax.axis_index("pen")
    width_x = CX * bins
    width_y = CY * pens
    channels = lift_input.shape[1]
    modes = spectral_weights.shape[0]
    points = features.shape[0]
    block = min(points, 1024)
    span_x = CX + 2
    span_y = CY + 2
    slots = jnp.arange(neighbours.shape[1], dtype=jnp.int32)[None, :]

    def add_block(step, grid):
        start = (step * block).astype(jnp.int32)
        codes = lax.dynamic_slice_in_dim(neighbours, start, block, 0)
        feat_rows = lax.dynamic_slice_in_dim(features, start, block, 0)
        where = lax.dynamic_slice_in_dim(positions, start, block, 1)
        home = lax.dynamic_slice_in_dim(home_cells, start, block, 1)
        live = lax.dynamic_slice_in_dim(degrees, start, block, 0)
        cell_x = jnp.clip(bin_index * CX + home[0][:, None] + codes // 9 - 1, 0, width_x - 1)
        cell_y = jnp.clip(pen_index * CY + home[1][:, None] + codes // 3 % 3 - 1, 0, width_y - 1)
        cell_z = jnp.clip(home[2][:, None] + codes % 3 - 1, 0, NZ - 1)
        off_x = cell_x.astype(jnp.float32) + 0.5 - where[0][:, None]
        off_y = cell_y.astype(jnp.float32) + 0.5 - where[1][:, None]
        off_z = cell_z.astype(jnp.float32) + 0.5 - where[2][:, None]
        valid = (slots < live[:, None]).astype(jnp.float32)
        message = pair_messages(
            off_x,
            off_y,
            off_z,
            feat_rows,
            valid,
            kernel_first,
            kernel_bias,
            kernel_second,
            lift_input,
        )
        local = (
            (cell_x - bin_index * CX + 1) * span_y + (cell_y - pen_index * CY + 1)
        ) * NZ + cell_z
        return grid.at[local.reshape(-1)].add(message.reshape(-1, channels))

    grid = lax.fori_loop(
        0, points // block, add_block, jnp.zeros((span_x * span_y * NZ, channels), jnp.float32)
    )
    grid = grid.reshape(span_x, span_y, NZ, channels)
    from_below = passed_along(grid[CX + 1], "bin", 1)
    from_above = passed_along(grid[0], "bin", -1)
    inner = grid[1 : CX + 1]
    inner = inner.at[0].add(from_below).at[CX - 1].add(from_above)
    from_left = passed_along(inner[:, CY + 1], "pen", 1)
    from_right = passed_along(inner[:, 0], "pen", -1)
    latent = inner[:, 1 : CY + 1]
    latent = latent.at[:, 0].add(from_left).at[:, CY - 1].add(from_right)
    cos_z, sin_z = dft_table(jnp.arange(NZ, dtype=jnp.int32), NZ, modes, False)
    cos_y, sin_y = dft_table(jnp.arange(width_y, dtype=jnp.int32), width_y, modes, True)
    z_re = jnp.einsum("xyzc,zk->xykc", latent, cos_z, precision=high)
    z_im = -jnp.einsum("xyzc,zk->xykc", latent, sin_z, precision=high)
    z_spec = jnp.stack([z_re, z_im], axis=3)
    y_in = lax.all_to_all(z_spec, "pen", split_axis=2, concat_axis=1, tiled=True)
    y_spec = forward_along(y_in, cos_y, sin_y, "xykc,yj->xjkc")
    x_in = lax.all_to_all(y_spec, "bin", split_axis=1, concat_axis=0, tiled=True)
    cos_x, sin_x = dft_table(jnp.arange(width_x, dtype=jnp.int32), width_x, modes, True)
    x_spec = forward_along(x_in, cos_x, sin_x, "xykc,xj->jykc")
    weights = spectral_weights.astype(jnp.float32)
    real_w = jnp.einsum("abki,abkio->abko", x_spec[:, :, :, 0], weights, precision=high)
    imag_w = jnp.einsum("abki,abkio->abko", x_spec[:, :, :, 1], weights, precision=high)
    mix_re = real_w[..., :channels] - imag_w[..., channels:]
    mix_im = real_w[..., channels:] + imag_w[..., :channels]
    mixed = jnp.stack([mix_re, mix_im], axis=3)
    own_rows = bin_index * CX + jnp.arange(CX, dtype=jnp.int32)
    own_cos, own_sin = dft_table(own_rows, width_x, modes, True)
    y_back = invert_along(
        lax.all_gather(mixed, "bin", axis=1, tiled=True), own_cos, own_sin, "jykc,xj->xykc"
    )
    y_rows = invert_along(y_back, cos_y, sin_y, "xjkc,yj->xykc")
    z_back = lax.all_to_all(y_rows, "pen", split_axis=1, concat_axis=2, tiled=True)
    doubling = jnp.where(jnp.arange(modes) == 0, 1.0, 2.0).astype(jnp.float32)[:, None]
    spectral_part = jnp.einsum(
        "xykc,zk->xyzc", z_back[:, :, :, 0] * doubling, cos_z, precision=high
    ) - jnp.einsum("xykc,zk->xyzc", z_back[:, :, :, 1] * doubling, sin_z, precision=high)
    skip = jnp.einsum("xyzc,cd->xyzd", latent, skip_weights, precision=high)
    return jax.nn.gelu(spectral_part + skip + skip_bias).astype(jnp.bfloat16)


def solution(mesh):
    in_specs = (
        P(("bin", "pen"), None),
        P(None, ("bin", "pen")),
        P(None, ("bin", "pen")),
        P(("bin", "pen"), None),
        P(("bin", "pen")),
        P(),
        P(),
        P(),
        P(),
        P(None, "bin", "pen", None, None),
        P(),
        P(),
    )
    out_specs = P("bin", "pen", None, None)
    return jax.shard_map(
        per_device, mesh=mesh, in_specs=in_specs, out_specs=out_specs, check_vma=False
    )
```

profile of v0, /device:TPU:32, one launch (start us, length us, event | category | flops | bytes accessed | tf_op | source)
XLA Modules:
  0.0 468.0 jit_solution(8501826001774433996)
XLA Ops:
  7.5 2.8 broadcast_in_dim.45
  10.3 199.2 %while.21 = (s32[]{:T(128)}, f32[11520,64]{1,0:T(8,128)}, s32[]{:T(128)}, s32[3,2048]{1,0:T(4,128)}, s32[2048,16]{0,1:T(8,128)S(1)}, /*index=5*/s32[]{:T(128)}, ...) while((s32[]{:T(128)}, f32[11520,64]{1,0:T(8,128)}, ...), condition=%wide.region_2.3_spmd.clone, body=%wide.region_0.2_spmd.clone.sunk | while | flops 162891776 | bytes 27241264 | solution.py:132
  12.7 4.4 multiply_multiply_fusion.4
  17.1 8.1 %copy.187 = f32[1024,16,64]{2,1,0:T(8,128)} copy(f32[1024,16,64]{0,2,1:T(8,128)} %multiply_multiply_fusion.4) | data formatting | bytes 8388608 | tf_op jit(solution)/shard_map/while/body/eval_jaxpr/mul | solution.py:44
  25.9 84.0 %scatter_fusion = f32[11520,64]{1,0:T(8,128)} fusion(f32[11520,64]{1,0:T(8,128)} %get-tuple-element.709, s32[16384]{0:T(1024)S(1)} %bitcast.259, f32[16384,64]{1,0:T(8,128)} %bitcast.253), kind=kCustom, calls=%fused_computation.clone.clone.1 | custom fusion | flops 1048576 | bytes 12648448 | tf_op jit(solution)/shard_map/while/body/eval_jaxpr/scatter-add | solution.py:130
  112.3 4.4 multiply_multiply_fusion.4
  116.7 8.1 %copy.187 = f32[1024,16,64]{2,1,0:T(8,128)} copy(f32[1024,16,64]{0,2,1:T(8,128)} %multiply_multiply_fusion.4) | data formatting | bytes 8388608 | tf_op jit(solution)/shard_map/while/body/eval_jaxpr/mul | solution.py:44
  125.5 84.0 %scatter_fusion = f32[11520,64]{1,0:T(8,128)} fusion(f32[11520,64]{1,0:T(8,128)} %get-tuple-element.709, s32[16384]{0:T(1024)S(1)} %bitcast.259, f32[16384,64]{1,0:T(8,128)} %bitcast.253), kind=kCustom, calls=%fused_computation.clone.clone.1 | custom fusion | flops 1048576 | bytes 12648448 | tf_op jit(solution)/shard_map/while/body/eval_jaxpr/scatter-add | solution.py:130
  209.5 2.9 fusion.244
  212.5 2.4 copy.115
  214.9 2.6 collective-permute-start
  217.5 1.2 copy.118
  218.7 1.3 collective-permute-start.1
  220.0 4.2 slice.269
  224.6 4.9 %copy.117 = f32[4,10,192,64]{2,3,0,1:T(8,128)} copy(f32[4,10,192,64]{3,2,1,0:T(8,128)} %bitcast.254) | data formatting | bytes 3932160 | tf_op jit(solution)/shard_map/slice | solution.py:138
  229.6 2.0 bitcast_dynamic-update-slice_fusion
  231.6 2.3 fusion.64
  233.9 1.1 slice_bitcast_fusion.17
  234.9 3.8 collective-permute-start.2
  238.8 1.7 slice.302
  240.5 4.9 %collective-permute-start.3 = (f32[4,192,64]{1,2,0:T(8,128)S(1)}, f32[4,192,64]{1,2,0:T(8,128)S(1)}, u32[]{:S(2)}, u32[]{:S(2)}) collective-permute-start(f32[4,192,64]{1,2,0:T(8,128)S(1)} %get-tuple-element.576), channel_id=1, source_target_pairs={{1,0},{2,1},{3,2},{4,3},{5,4},{6,5},{7,6},{8,7},{9,8},{10,9},{11,1... | collective-permute-start | bytes 589832 | tf_op jit(solution)/shard_map/ppermute | solution.py:15
  245.4 2.6 collective-permute-done.2
  248.0 1.0 fusion.75
  249.2 2.3 collective-permute-done.3
  251.5 3.1 convolution_bitcast_fusion
  254.6 3.1 fusion.51
  257.8 1.6 copy.182
  259.3 2.7 reshape.430
  262.0 14.9 %all-to-all-start = ((f32[16,1,8192]{2,1,0:T(1,128)}), f32[16,1,8192]{2,1,0:T(1,128)}, u32[]{:S(2)}, u32[]{:S(2)}) async-start(f32[16,1,8192]{2,1,0:T(1,128)} %reshape.430), calls=%async_computation | async-start | bytes 1048576 | tf_op jit(solution)/shard_map/all_to_all | solution.py:149
  277.0 29.1 %all-to-all-done = f32[16,1,8192]{2,1,0:T(1,128)} async-done(((f32[16,1,8192]{2,1,0:T(1,128)}), f32[16,1,8192]{2,1,0:T(1,128)}, u32[]{:S(2)}, u32[]{:S(2)}) %all-to-all-start) | async-done | bytes 524320 | tf_op jit(solution)/shard_map/all_to_all | solution.py:149
  306.6 3.7 reduce.8
  310.2 2.4 reshape.431
  312.7 1.3 copy.181
  316.6 14.8 %all_to_all.54 = f32[32,1,1024]{2,1,0:T(1,128)S(1)} all-to-all(f32[32,1,1024]{2,1,0:T(1,128)S(1)} %reshape.432), channel_id=1, replica_groups=mesh['bin'=32,'pen'=16] {'bin'}, dimensions={0} | all-to-all | bytes 262144 | tf_op jit(solution)/shard_map/all_to_all | solution.py:151
  334.7 0.9 fusion.58
  336.4 51.5 %all-gather.2.cloned.1.call-done = f32[32,32,2,2,64]{4,0,2,1,3:T(8,128)} async-done(((f32[32,1,2,2,64]{4,0,2,1,3:T(8,128)}), f32[32,32,2,2,64]{4,0,2,1,3:T(8,128)}) %all-gather.2.cloned.1.call-update) | async-done | bytes 1048592 | tf_op jit(solution)/shard_map/all_gather | solution.py:163
  387.9 2.0 fusion.62
  390.0 1.9 convolution_subtract_fusion.2
  396.7 2.2 copy.134
  398.9 3.1 reshape.434
  402.0 13.0 %all-to-all-start.2 = ((f32[16,1,8192]{2,1,0:T(1,128)}), f32[16,1,8192]{2,1,0:T(1,128)}, u32[]{:S(2)}, u32[]{:S(2)}) async-start(f32[16,1,8192]{2,1,0:T(1,128)} %reshape.434), calls=%async_computation.2 | async-start | bytes 1048576 | tf_op jit(solution)/shard_map/all_to_all | solution.py:166
  415.1 29.6 %all-to-all-done.2 = f32[16,1,8192]{2,1,0:T(1,128)} async-done(((f32[16,1,8192]{2,1,0:T(1,128)}), f32[16,1,8192]{2,1,0:T(1,128)}, u32[]{:S(2)}, u32[]{:S(2)}) %all-to-all-start.2) | async-done | bytes 524320 | tf_op jit(solution)/shard_map/all_to_all | solution.py:166
  444.7 3.7 reduce.10
  448.4 2.8 reshape.435
  451.1 1.6 copy.180
  453.0 2.0 fusion.67
  455.0 2.0 fusion.69
  457.0 3.9 fusion.49
  (85 shorter events, 19.8 us)
Async XLA Ops:
  6.5 327.3 %copy-start = (bf16[32,1,2,64,128]{4,3,2,1,0:T(8,128)(2,1)S(1)}, bf16[32,1,2,64,128]{4,3,2,1,0:T(8,128)(2,1)}, u32[]{:S(2)}) copy-start(bf16[32,1,2,64,128]{4,3,2,1,0:T(8,128)(2,1)} %param.31) | copy-start | bytes 3145732
  7.4 2.8 copy-start.2
  7.4 2.8 copy-start.3
  7.5 2.8 copy-start.4
  7.5 2.8 copy-start.5
  7.5 2.8 copy-start.7
  7.5 2.8 copy-start.9
  214.9 14.7 %collective-permute-start = (f32[10,192,64]{1,2,0:T(8,128)}, f32[10,192,64]{1,2,0:T(8,128)}, u32[]{:S(2)}, u32[]{:S(2)}) collective-permute-start(f32[10,192,64]{1,2,0:T(8,128)} %copy.115), channel_id=1, source_target_pairs={{0,16},{16,32},{32,48},{48,64},{64,80},{80,96},{96,112},{112,128},... | collective-permute-start | bytes 1474568 | tf_op jit(solution)/shard_map/ppermute | solution.py:15
  218.7 12.9 %collective-permute-start.1 = (f32[10,192,64]{1,2,0:T(8,128)}, f32[10,192,64]{1,2,0:T(8,128)}, u32[]{:S(2)}, u32[]{:S(2)}) collective-permute-start(f32[10,192,64]{1,2,0:T(8,128)} %copy.118), channel_id=1, source_target_pairs={{16,0},{32,16},{48,32},{64,48},{80,64},{96,80},{112,96},{128,112},... | collective-permute-start | bytes 1474568 | tf_op jit(solution)/shard_map/ppermute | solution.py:15
  234.9 13.1 %collective-permute-start.2 = (f32[4,192,64]{1,2,0:T(8,128)S(1)}, f32[4,192,64]{1,2,0:T(8,128)S(1)}, u32[]{:S(2)}, u32[]{:S(2)}) collective-permute-start(f32[4,192,64]{1,2,0:T(8,128)S(1)} %get-tuple-element.577), channel_id=1, source_target_pairs={{0,1},{1,2},{2,3},{3,4},{4,5},{5,6},{6,7},{7,8},{8,9},{9,10},{10,1... | collective-permute-start | bytes 589832 | tf_op jit(solution)/shard_map/ppermute | solution.py:15
  240.5 10.9 %collective-permute-start.3 = (f32[4,192,64]{1,2,0:T(8,128)S(1)}, f32[4,192,64]{1,2,0:T(8,128)S(1)}, u32[]{:S(2)}, u32[]{:S(2)}) collective-permute-start(f32[4,192,64]{1,2,0:T(8,128)S(1)} %get-tuple-element.576), channel_id=1, source_target_pairs={{1,0},{2,1},{3,2},{4,3},{5,4},{6,5},{7,6},{8,7},{9,8},{10,9},{11,1... | collective-permute-start | bytes 589832 | tf_op jit(solution)/shard_map/ppermute | solution.py:15
  262.0 44.0 %all-to-all-start = ((f32[16,1,8192]{2,1,0:T(1,128)}), f32[16,1,8192]{2,1,0:T(1,128)}, u32[]{:S(2)}, u32[]{:S(2)}) async-start(f32[16,1,8192]{2,1,0:T(1,128)} %reshape.430), calls=%async_computation | async-start | bytes 1048576 | tf_op jit(solution)/shard_map/all_to_all | solution.py:149
  276.9 111.0 %all-gather.2.cloned.1.call-start = ((), (), s32[]{:S(2)}) async-start(), calls=%async_computation.3 | async-start | bytes 2162688 | tf_op jit(solution)/shard_map/all_gather | solution.py:163
  387.9 4.6 copy-start.1
  402.0 42.7 %all-to-all-start.2 = ((f32[16,1,8192]{2,1,0:T(1,128)}), f32[16,1,8192]{2,1,0:T(1,128)}, u32[]{:S(2)}, u32[]{:S(2)}) async-start(f32[16,1,8192]{2,1,0:T(1,128)} %reshape.434), calls=%async_computation.2 | async-start | bytes 1048576 | tf_op jit(solution)/shard_map/all_to_all | solution.py:166
  453.0 4.0 copy-start.6
  453.0 4.0 copy-start.8
Sparse Core Ops, SparseCore 0:
  336.6 51.3 all-gather.1
where the time goes:
time: 476 us; the launch traced here: 468 us
  other arithmetic  186 us (39%)
  waiting for transfers between devices  115 us (24%)
  local copies, waits for them, and re-layouts  60.7 us (13%)
  starting transfers between devices  40.5 us (9%)
  matrix products  36.4 us (8%)
  blocking collectives  14.8 us (3%)
  between operations  14.1 us (3%)
    scatter-add x2, other arithmetic, add_block(): return grid.at[local.reshape(-1)].add(message.reshape(-1, channels))  168 us
    all_gather x1, waiting for transfers between devices, per_device(): lax.all_gather(mixed, 'bin', axis=1, tiled=True)  51.5 us
    all_to_all x1, waiting for transfers between devices, per_device(): lax.all_to_all(y_rows, 'pen', split_axis=1, concat_axis=2, tiled=True)  29.6 us
    all_to_all x1, waiting for transfers between devices, per_device(): lax.all_to_all(z_spec, 'pen', split_axis=2, concat_axis=1, tiled=True)  29.1 us
    mul x2, local copies, waits for them, and re-layouts, pair_messages(): return kernel * values[:, None, :] * valid[..., None]  16.2 us
    all_to_all x1, starting transfers between devices, per_device(): lax.all_to_all(z_spec, 'pen', split_axis=2, concat_axis=1, tiled=True)  14.9 us
    all_to_all x1, blocking collectives, per_device(): lax.all_to_all(y_spec, 'bin', split_axis=1, concat_axis=0, tiled=True)  14.8 us
    all_to_all x1, starting transfers between devices, per_device(): lax.all_to_all(y_rows, 'pen', split_axis=1, concat_axis=2, tiled=True)  13 us
  transfers between devices with their start and end apart: 7, of which 5 were waited for; matrix products, arithmetic and copies ran while one was open for 3% of the time, Pallas kernels for 0%

commit v1 on v0

--- a/solution.py
+++ b/solution.py
@@ -160,7 +160,12 @@
     own_rows = bin_index * CX + jnp.arange(CX, dtype=jnp.int32)
     own_cos, own_sin = dft_table(own_rows, width_x, modes, True)
     y_back = invert_along(
-        lax.all_gather(mixed, "bin", axis=1, tiled=True), own_cos, own_sin, "jykc,xj->xykc"
+        jnp.concatenate(
+            lax.all_to_all(jnp.stack([mixed] * lax.axis_size("bin")), "bin", 0, 0), axis=1
+        ),
+        own_cos,
+        own_sin,
+        "jykc,xj->xykc",
     )
     y_rows = invert_along(y_back, cos_y, sin_y, "xjkc,yj->xykc")
     z_back = lax.all_to_all(y_rows, "pen", split_axis=1, concat_axis=2, tiled=True)

time: 476 us -> 439 us (0.922)
  waiting for transfers between devices: 115 us -> 80.6 us
  between operations: 14.1 us -> 0.73 us
  local copies, waits for them, and re-layouts: 60.7 us -> 70.7 us
  other arithmetic: 186 us -> 191 us
    all_gather x1 -> x0, waiting for transfers between devices: 51.5 us -> none  [per_device(): lax.all_gather(mixed, 'bin', axis=1, tiled=True)]
    all_to_all x0 -> x1, waiting for transfers between devices: none -> 17.3 us  [per_device(): lax.all_to_all(jnp.stack([mixed] * lax.axis_size('bin')), 'bin', 0, 0)]
    unnamed x27 -> x28, local copies, waits for them, and re-layouts: 12.4 us -> 20.5 us
    all_to_all x1, starting transfers between devices: 13 us -> 7.64 us  [per_device(): lax.all_to_all(y_rows, 'pen', split_axis=1, concat_axis=2, tiled=True)]
    all_to_all x0 -> x1, other arithmetic: none -> 5.33 us  [per_device(): lax.all_to_all(jnp.stack([mixed] * lax.axis_size('bin')), 'bin', 0, 0)]
    all_to_all x0 -> x1, starting transfers between devices: none -> 4.83 us  [per_device(): lax.all_to_all(jnp.stack([mixed] * lax.axis_size('bin')), 'bin', 0, 0)]
  transfers between devices with their start and end apart: 7 -> 7, of which waited for: 5 -> 5; matrix products, arithmetic and copies ran while one was open for 3% -> 4% of each run, Pallas kernels for 0% -> 0%
where the time goes in v1:
time: 439 us; the launch traced here: 431 us
  other arithmetic  191 us (44%)
  waiting for transfers between devices  80.6 us (18%)
  local copies, waits for them, and re-layouts  70.7 us (16%)
  starting transfers between devices  39.9 us (9%)
  matrix products  33.9 us (8%)
  blocking collectives  14.1 us (3%)
    scatter-add x2, other arithmetic, add_block(): return grid.at[local.reshape(-1)].add(message.reshape(-1, channels))  168 us
    all_to_all x1, waiting for transfers between devices, per_device(): lax.all_to_all(z_spec, 'pen', split_axis=2, concat_axis=1, tiled=True)  29.4 us
    all_to_all x1, waiting for transfers between devices, per_device(): lax.all_to_all(y_rows, 'pen', split_axis=1, concat_axis=2, tiled=True)  28.9 us
    unnamed x28, local copies, waits for them, and re-layouts  20.5 us
    all_to_all x1, waiting for transfers between devices, per_device(): lax.all_to_all(jnp.stack([mixed] * lax.axis_size('bin')), 'bin', 0, 0)  17.3 us
    mul x2, local copies, waits for them, and re-layouts, pair_messages(): return kernel * values[:, None, :] * valid[..., None]  16.2 us
    all_to_all x1, starting transfers between devices, per_device(): lax.all_to_all(z_spec, 'pen', split_axis=2, concat_axis=1, tiled=True)  14.9 us
    all_to_all x1, blocking collectives, per_device(): lax.all_to_all(y_spec, 'bin', split_axis=1, concat_axis=0, tiled=True)  14.1 us
  transfers between devices with their start and end apart: 7, of which 5 were waited for; matrix products, arithmetic and copies ran while one was open for 4% of the time, Pallas kernels for 0%

profile of v1, /device:TPU:32, one launch (start us, length us, event | category | flops | bytes accessed | tf_op | source)
XLA Modules:
  0.0 431.0 jit_solution(9092775710601189341)
XLA Ops:
  1.0 2.8 broadcast_in_dim.45
  3.8 199.3 %while.21 = (s32[]{:T(128)}, f32[11520,64]{1,0:T(8,128)}, s32[]{:T(128)}, s32[3,2048]{1,0:T(4,128)}, s32[2048,16]{0,1:T(8,128)S(1)}, /*index=5*/s32[]{:T(128)}, ...) while((s32[]{:T(128)}, f32[11520,64]{1,0:T(8,128)}, ...), condition=%wide.region_2.3_spmd.clone, body=%wide.region_0.2_spmd.clone.sunk | while | flops 162891776 | bytes 27241264 | solution.py:132
  6.2 4.5 %multiply_multiply_fusion.4 = f32[1024,16,64]{0,2,1:T(8,128)} fusion(f32[1024,16]{0,1:T(8,128)S(1)} %fusion.262, f32[1024,64]{0,1:T(8,128)S(1)} %fusion.263, f32[64]{0:T(128)S(1)} %get-tuple-element.735, f32[64]{0:T(128)S(1)} %get-tuple-element.681, f32[1024,16]{0,1:T(8,128)S(1)} %get-tuple-element.684, f32[64]{0:T(128)S(1)} %get-tuple-element.685, ...), kind=kOutput, calls=%fused_computation.11.clone.1 | convolution fusion | flops 152043520 | bytes 4727808 | tf_op jit(solution)/shard_map/while/body/eval_jaxpr/dot_general | solution.py:39
  10.7 8.1 %copy.185 = f32[1024,16,64]{2,1,0:T(8,128)} copy(f32[1024,16,64]{0,2,1:T(8,128)} %multiply_multiply_fusion.4) | data formatting | bytes 8388608 | tf_op jit(solution)/shard_map/while/body/eval_jaxpr/mul | solution.py:44
  19.5 84.0 %scatter_fusion = f32[11520,64]{1,0:T(8,128)} fusion(f32[11520,64]{1,0:T(8,128)} %get-tuple-element.709, s32[16384]{0:T(1024)S(1)} %bitcast.268, f32[16384,64]{1,0:T(8,128)} %bitcast.262), kind=kCustom, calls=%fused_computation.clone.clone.1 | custom fusion | flops 1048576 | bytes 12648448 | tf_op jit(solution)/shard_map/while/body/eval_jaxpr/scatter-add | solution.py:130
  105.8 4.5 %multiply_multiply_fusion.4 = f32[1024,16,64]{0,2,1:T(8,128)} fusion(f32[1024,16]{0,1:T(8,128)S(1)} %fusion.262, f32[1024,64]{0,1:T(8,128)S(1)} %fusion.263, f32[64]{0:T(128)S(1)} %get-tuple-element.735, f32[64]{0:T(128)S(1)} %get-tuple-element.681, f32[1024,16]{0,1:T(8,128)S(1)} %get-tuple-element.684, f32[64]{0:T(128)S(1)} %get-tuple-element.685, ...), kind=kOutput, calls=%fused_computation.11.clone.1 | convolution fusion | flops 152043520 | bytes 4727808 | tf_op jit(solution)/shard_map/while/body/eval_jaxpr/dot_general | solution.py:39
  110.3 8.1 %copy.185 = f32[1024,16,64]{2,1,0:T(8,128)} copy(f32[1024,16,64]{0,2,1:T(8,128)} %multiply_multiply_fusion.4) | data formatting | bytes 8388608 | tf_op jit(solution)/shard_map/while/body/eval_jaxpr/mul | solution.py:44
  119.1 84.0 %scatter_fusion = f32[11520,64]{1,0:T(8,128)} fusion(f32[11520,64]{1,0:T(8,128)} %get-tuple-element.709, s32[16384]{0:T(1024)S(1)} %bitcast.268, f32[16384,64]{1,0:T(8,128)} %bitcast.262), kind=kCustom, calls=%fused_computation.clone.clone.1 | custom fusion | flops 1048576 | bytes 12648448 | tf_op jit(solution)/shard_map/while/body/eval_jaxpr/scatter-add | solution.py:130
  203.1 2.9 fusion.244
  206.0 2.4 copy.112
  208.5 2.6 collective-permute-start
  212.3 1.3 collective-permute-start.1
  213.6 4.2 slice.269
  218.2 4.9 %copy.114 = f32[4,10,192,64]{2,3,0,1:T(8,128)} copy(f32[4,10,192,64]{3,2,1,0:T(8,128)} %bitcast.263) | data formatting | bytes 3932160 | tf_op jit(solution)/shard_map/slice | solution.py:138
  223.1 2.0 bitcast_dynamic-update-slice_fusion
  225.1 2.2 fusion.64
  228.4 3.8 collective-permute-start.2
  232.3 1.7 slice.302
  234.0 4.9 %collective-permute-start.3 = (f32[4,192,64]{1,2,0:T(8,128)S(1)}, f32[4,192,64]{1,2,0:T(8,128)S(1)}, u32[]{:S(2)}, u32[]{:S(2)}) collective-permute-start(f32[4,192,64]{1,2,0:T(8,128)S(1)} %get-tuple-element.576), channel_id=1, source_target_pairs={{1,0},{2,1},{3,2},{4,3},{5,4},{6,5},{7,6},{8,7},{9,8},{10,9},{11,1... | collective-permute-start | bytes 589832 | tf_op jit(solution)/shard_map/ppermute | solution.py:15
  238.9 2.6 collective-permute-done.2
  242.7 2.3 collective-permute-done.3
  245.0 3.1 convolution_bitcast_fusion
  248.1 3.1 fusion.51
  251.3 1.6 copy.180
  252.8 2.7 reshape.441
  255.5 14.9 %all-to-all-start = ((f32[16,1,8192]{2,1,0:T(1,128)}), f32[16,1,8192]{2,1,0:T(1,128)}, u32[]{:S(2)}, u32[]{:S(2)}) async-start(f32[16,1,8192]{2,1,0:T(1,128)} %reshape.441), calls=%async_computation | async-start | bytes 1048576 | tf_op jit(solution)/shard_map/all_to_all | solution.py:149
  270.4 29.4 %all-to-all-done = f32[16,1,8192]{2,1,0:T(1,128)} async-done(((f32[16,1,8192]{2,1,0:T(1,128)}), f32[16,1,8192]{2,1,0:T(1,128)}, u32[]{:S(2)}, u32[]{:S(2)}) %all-to-all-start) | async-done | bytes 524320 | tf_op jit(solution)/shard_map/all_to_all | solution.py:149
  300.4 3.7 reduce.8
  304.0 2.4 reshape.442
  306.5 1.3 copy.179
  310.4 14.1 %all_to_all.59 = f32[32,1,1024]{2,1,0:T(1,128)S(1)} all-to-all(f32[32,1,1024]{2,1,0:T(1,128)S(1)} %reshape.443), channel_id=1, replica_groups=mesh['bin'=32,'pen'=16] {'bin'}, dimensions={0} | all-to-all | bytes 262144 | tf_op jit(solution)/shard_map/all_to_all | solution.py:151
  328.9 1.6 broadcast_bitcast_fusion
  330.5 3.4 reshape.445
  333.9 4.8 %all-to-all-start.2 = ((f32[32,1,8192]{2,1,0:T(1,128)}), f32[32,1,8192]{2,1,0:T(1,128)}, u32[]{:S(2)}, u32[]{:S(2)}) async-start(f32[32,1,8192]{2,1,0:T(1,128)} %reshape.445), calls=%async_computation.2 | async-start | bytes 2097152 | tf_op jit(solution)/shard_map/all_to_all | solution.py:164
  338.8 17.3 %all-to-all-done.2 = f32[32,1,8192]{2,1,0:T(1,128)} async-done(((f32[32,1,8192]{2,1,0:T(1,128)}), f32[32,1,8192]{2,1,0:T(1,128)}, u32[]{:S(2)}, u32[]{:S(2)}) %all-to-all-start.2) | async-done | bytes 1048608 | tf_op jit(solution)/shard_map/all_to_all | solution.py:164
  356.1 5.3 %reduce.10 = f32[32,8192]{1,0:T(8,128)} reduce(f32[32,1,8192]{2,1,0:T(1,128)} %all-to-all-done.2, f32[]{:T(128)} %broadcast.649), dimensions={1}, to_apply=%all_to_all.50.reduce_sub_computation | reduce | bytes 2097156 | tf_op jit(solution)/shard_map/all_to_all | solution.py:164
  361.5 3.1 reshape.446
  364.6 1.8 copy_bitcast_fusion
  372.6 2.2 copy.131
  374.8 3.1 reshape.447
  377.9 7.6 %all-to-all-start.3 = ((f32[16,1,8192]{2,1,0:T(1,128)}), f32[16,1,8192]{2,1,0:T(1,128)}, u32[]{:S(2)}, u32[]{:S(2)}) async-start(f32[16,1,8192]{2,1,0:T(1,128)} %reshape.447), calls=%async_computation.3 | async-start | bytes 1048576 | tf_op jit(solution)/shard_map/all_to_all | solution.py:171
  385.6 28.9 %all-to-all-done.3 = f32[16,1,8192]{2,1,0:T(1,128)} async-done(((f32[16,1,8192]{2,1,0:T(1,128)}), f32[16,1,8192]{2,1,0:T(1,128)}, u32[]{:S(2)}, u32[]{:S(2)}) %all-to-all-start.3) | async-done | bytes 524320 | tf_op jit(solution)/shard_map/all_to_all | solution.py:171
  414.5 3.7 reduce.11
  418.2 2.8 reshape.448
  420.9 1.6 copy.178
  422.8 2.0 fusion.67
  424.8 2.0 fusion.69
  426.8 3.9 fusion.49
  (87 shorter events, 24.7 us)
Async XLA Ops:
  0.0 326.9 %copy-start = (bf16[32,1,2,64,128]{4,3,2,1,0:T(8,128)(2,1)S(1)}, bf16[32,1,2,64,128]{4,3,2,1,0:T(8,128)(2,1)}, u32[]{:S(2)}) copy-start(bf16[32,1,2,64,128]{4,3,2,1,0:T(8,128)(2,1)} %param.31) | copy-start | bytes 3145732
  0.9 2.9 copy-start.1
  0.9 2.8 copy-start.2
  0.9 2.8 copy-start.3
  0.9 2.8 copy-start.4
  0.9 2.8 copy-start.6
  1.0 2.8 copy-start.8
  208.5 14.6 %collective-permute-start = (f32[10,192,64]{1,2,0:T(8,128)}, f32[10,192,64]{1,2,0:T(8,128)}, u32[]{:S(2)}, u32[]{:S(2)}) collective-permute-start(f32[10,192,64]{1,2,0:T(8,128)} %copy.112), channel_id=1, source_target_pairs={{0,16},{16,32},{32,48},{48,64},{64,80},{80,96},{96,112},{112,128},... | collective-permute-start | bytes 1474568 | tf_op jit(solution)/shard_map/ppermute | solution.py:15
  212.3 12.9 %collective-permute-start.1 = (f32[10,192,64]{1,2,0:T(8,128)}, f32[10,192,64]{1,2,0:T(8,128)}, u32[]{:S(2)}, u32[]{:S(2)}) collective-permute-start(f32[10,192,64]{1,2,0:T(8,128)} %copy.115), channel_id=1, source_target_pairs={{16,0},{32,16},{48,32},{64,48},{80,64},{96,80},{112,96},{128,112},... | collective-permute-start | bytes 1474568 | tf_op jit(solution)/shard_map/ppermute | solution.py:15
  228.4 13.1 %collective-permute-start.2 = (f32[4,192,64]{1,2,0:T(8,128)S(1)}, f32[4,192,64]{1,2,0:T(8,128)S(1)}, u32[]{:S(2)}, u32[]{:S(2)}) collective-permute-start(f32[4,192,64]{1,2,0:T(8,128)S(1)} %get-tuple-element.577), channel_id=1, source_target_pairs={{0,1},{1,2},{2,3},{3,4},{4,5},{5,6},{6,7},{7,8},{8,9},{9,10},{10,1... | collective-permute-start | bytes 589832 | tf_op jit(solution)/shard_map/ppermute | solution.py:15
  234.0 10.9 %collective-permute-start.3 = (f32[4,192,64]{1,2,0:T(8,128)S(1)}, f32[4,192,64]{1,2,0:T(8,128)S(1)}, u32[]{:S(2)}, u32[]{:S(2)}) collective-permute-start(f32[4,192,64]{1,2,0:T(8,128)S(1)} %get-tuple-element.576), channel_id=1, source_target_pairs={{1,0},{2,1},{3,2},{4,3},{5,4},{6,5},{7,6},{8,7},{9,8},{10,9},{11,1... | collective-permute-start | bytes 589832 | tf_op jit(solution)/shard_map/ppermute | solution.py:15
  255.5 44.3 %all-to-all-start = ((f32[16,1,8192]{2,1,0:T(1,128)}), f32[16,1,8192]{2,1,0:T(1,128)}, u32[]{:S(2)}, u32[]{:S(2)}) async-start(f32[16,1,8192]{2,1,0:T(1,128)} %reshape.441), calls=%async_computation | async-start | bytes 1048576 | tf_op jit(solution)/shard_map/all_to_all | solution.py:149
  333.9 22.2 %all-to-all-start.2 = ((f32[32,1,8192]{2,1,0:T(1,128)}), f32[32,1,8192]{2,1,0:T(1,128)}, u32[]{:S(2)}, u32[]{:S(2)}) async-start(f32[32,1,8192]{2,1,0:T(1,128)} %reshape.445), calls=%async_computation.2 | async-start | bytes 2097152 | tf_op jit(solution)/shard_map/all_to_all | solution.py:164
  377.9 36.6 %all-to-all-start.3 = ((f32[16,1,8192]{2,1,0:T(1,128)}), f32[16,1,8192]{2,1,0:T(1,128)}, u32[]{:S(2)}, u32[]{:S(2)}) async-start(f32[16,1,8192]{2,1,0:T(1,128)} %reshape.447), calls=%async_computation.3 | async-start | bytes 1048576 | tf_op jit(solution)/shard_map/all_to_all | solution.py:171
  422.8 4.0 copy-start.5
  422.8 4.0 copy-start.7
